TPU v7x, 32 devices: a whole 2x2x4 slice. The times are simulated.
32 devices in a mesh: dp: 4 (over x, core), seq: 8 (over z, y).
Axes of the slice: x: 2, y: 2, z: 4, core: 2. Of those that a mesh axis runs over, the one named last changes fastest.
Arguments:
- grad_out: bfloat16 [4, 64, 8192], P('dp', None, 'seq'), may hold values from -6 to 6
- gate: bfloat16 [4, 64, 8192], P('dp', None, 'seq'), may hold values from -6 to 6
- input_spectrum: float32 [4, 2, 64, 8192], P('dp', None, None, 'seq'), may hold values from -6 to 6
- filter_spectrum: float32 [2, 64, 8192], P(None, 'dp', 'seq'), may hold values from -6 to 6
Outputs:
- grad_input: bfloat16 [4, 64, 8192], P('dp', None, 'seq')
- grad_gate: bfloat16 [4, 64, 8192], P('dp', None, 'seq')
- grad_filter: float32 [2, 64, 8192], P(None, 'dp', 'seq')
All inputs are finite; a program needn't handle non-finite values.
Results may differ from a plain program's by a relative error of at most 0.002.
Values sent between devices are 32-bit elements; how exact they have to be, the bound alone decides.
A program may use at most 64 MiB of HBM per device.

v0:
```python
import math

import jax
import jax.numpy as jnp
import numpy as np
from jax import lax
from jax.sharding import PartitionSpec as P


def host_split(table):
    high = table.astype(jnp.bfloat16)
    low = (table - high.astype(np.float64)).astype(jnp.bfloat16)
    return high, low


def host_tables(seq_count, positions):
    index = np.arange(positions, dtype=np.int64)
    angle = (index[:, None] * index[None, :] % positions) * (2.0 * math.pi / positions)
    total_len = positions * seq_count
    classes = np.arange(seq_count, dtype=np.int64)
    turn = (classes[:, None] * index[None, :] % total_len) * (2.0 * math.pi / total_len)
    small = (classes[:, None] * classes[None, :] % seq_count) * (2.0 * math.pi / seq_count)
    scale = 1.0 / math.sqrt(total_len)
    return (
        host_split(np.cos(angle)),
        host_split(np.sin(angle)),
        ((np.cos(turn) * scale).astype(np.float32), (np.sin(turn) * scale).astype(np.float32)),
        (np.cos(small).astype(np.float32), np.sin(small).astype(np.float32)),
    )


def split_product(values, table):
    high = lax.reduce_precision(values, 8, 7)
    low = (values - high).astype(jnp.bfloat16)
    high = high.astype(jnp.bfloat16)
    rows = values.shape[0]
    both = jnp.dot(
        jnp.concatenate([high, low], axis=0), table[0], preferred_element_type=jnp.float32
    )
    rest = jnp.dot(high, table[1], preferred_element_type=jnp.float32)
    return both[:rows] + both[rows:] + rest


def mixed(matrix, blocks):
    return jnp.einsum(
        "fp,pcq->fcq",
        matrix,
        blocks,
        precision=lax.Precision.HIGHEST,
        preferred_element_type=jnp.float32,
    )


def per_device_arrays(grad_out, gate, input_spectrum, filter_spectrum, tables):
    batch, channels, positions = grad_out.shape
    seq_count = lax.axis_size("seq")
    own = channels // seq_count
    cos_table, sin_table, (tw_cos, tw_sin), (small_cos, small_sin) = tables
    tw_cos = tw_cos[None, :, None, :]
    tw_sin = tw_sin[None, :, None, :]

    def exchange(blocks):
        return lax.all_to_all(blocks, "seq", split_axis=1, concat_axis=1, tiled=True)

    def by_block(array):
        return array.reshape((array.shape[0], seq_count, own, positions))

    def transform(real, imag):
        shape = real.shape
        stacked = jnp.concatenate([real.reshape(-1, positions), imag.reshape(-1, positions)])
        rows = stacked.shape[0] // 2
        by_cos = split_product(stacked, cos_table)
        by_sin = split_product(stacked, sin_table)
        pick = lambda part, half: part[half * rows : (half + 1) * rows].reshape(shape)
        return pick(by_cos, 0), pick(by_cos, 1), pick(by_sin, 0), pick(by_sin, 1)

    def inverse(real, imag):
        rc, ic, rs, is_ = transform(real, imag)
        local_real, local_imag = rc - is_, ic + rs
        turned_real = local_real * tw_cos - local_imag * tw_sin
        turned_imag = local_imag * tw_cos + local_real * tw_sin
        return jax.vmap(
            lambda a, b: mixed(small_cos, a) - mixed(small_sin, b)
        )(turned_real, turned_imag)

    upstream = grad_out.astype(jnp.float32)
    delta = by_block(exchange(upstream * gate.astype(jnp.float32)))
    filters = lax.all_gather(filter_spectrum, "dp", axis=1, tiled=True)
    spectra = exchange(
        jnp.concatenate([input_spectrum.reshape((-1,) + input_spectrum.shape[2:]), filters])
    )
    spectra = by_block(spectra)
    in_real, in_imag = spectra[0 : 2 * batch : 2], spectra[1 : 2 * batch : 2]
    filt_real, filt_imag = spectra[2 * batch], spectra[2 * batch + 1]

    part_real = jax.vmap(lambda a: mixed(small_cos, a))(delta)
    part_imag = -jax.vmap(lambda a: mixed(small_sin, a))(delta)
    turned_real = part_real * tw_cos + part_imag * tw_sin
    turned_imag = part_imag * tw_cos - part_real * tw_sin
    rc, ic, rs, is_ = transform(turned_real, turned_imag)
    delta_real, delta_imag = rc + is_, ic - rs

    conv = inverse(
        in_real * filt_real - in_imag * filt_imag, in_real * filt_imag + in_imag * filt_real
    )
    backward = inverse(
        filt_real * delta_real + filt_imag * delta_imag,
        filt_real * delta_imag - filt_imag * delta_real,
    )
    term_real = jnp.sum(in_real * delta_real + in_imag * delta_imag, axis=0)
    term_imag = jnp.sum(in_real * delta_imag - in_imag * delta_real, axis=0)
    results = jnp.concatenate([conv, backward, jnp.stack([term_real, term_imag])])
    results = exchange(results.reshape(-1, channels, positions))
    conv, backward, terms = (
        results[:batch],
        results[batch : 2 * batch],
        results[2 * batch :],
    )
    grad_filter = lax.psum_scatter(terms, "dp", scatter_dimension=1, tiled=True)
    conv, backward = lax.optimization_barrier((conv, backward))
    return (
        backward.astype(jnp.bfloat16),
        (upstream * conv).astype(jnp.bfloat16),
        grad_filter,
    )


def solution(mesh):
    def per_device(grad_out, gate, input_spectrum, filter_spectrum):
        tables = host_tables(mesh.shape["seq"], grad_out.shape[2])
        return per_device_arrays(grad_out, gate, input_spectrum, filter_spectrum, tables)

    return jax.shard_map(
        per_device,
        mesh=mesh,
        in_specs=(
            P("dp", None, "seq"),
            P("dp", None, "seq"),
            P("dp", None, None, "seq"),
            P(None, "dp", "seq"),
        ),
        out_specs=(P("dp", None, "seq"), P("dp", None, "seq"), P(None, "dp", "seq")),
        check_vma=False,
    )
```

profile of v0, /device:TPU:0, one launch (start us, length us, event | category | flops | bytes accessed | tf_op | source)
XLA Modules:
  0.0 144.6 jit_solution(14777345282818017786)
XLA Ops:
  7.2 1.9 %fusion.20 = f32[1,64,1024]{2,0,1:T(1,128)} fusion(bf16[1,64,1024]{2,1,0:T(8,128)(2,1)} %param.17, bf16[1,64,1024]{2,1,0:T(8,128)(2,1)} %param.16), kind=kLoop, calls=%fused_computation.71 | loop fusion | flops 196608 | bytes 524288 | tf_op jit(solution)/shard_map/mul | solution.py:87
  9.1 7.3 %all-to-all-start.1 = ((f32[1,64,1024]{2,0,1:T(1,128)}), f32[1,64,1024]{2,0,1:T(1,128)S(1)}, u32[]{:S(2)}, u32[]{:S(2)}) async-start(f32[1,64,1024]{2,0,1:T(1,128)} %fusion.20), calls=%async_computation.1 | async-start | bytes 524288 | tf_op jit(solution)/shard_map/all_to_all | solution.py:63
  16.4 1.0 copy.65
  17.4 1.4 %copy.173 = f32[1,2,64,1024]{3,1,2,0:T(2,128)S(1)} copy(f32[1,2,64,1024]{3,2,1,0:T(8,128)} %param.18) | data formatting | bytes 1048576 | tf_op args[2]
  18.8 7.2 %all_gather.3 = f32[2,64,1024]{2,0,1:T(2,128)S(1)} all-gather(f32[2,16,1024]{2,0,1:T(2,128)S(1)} %copy.65), channel_id=1, replica_groups=mesh['dp'=4,'seq'=8] {'dp'}, dimensions={1}, use_global_device_ids=true | all-gather | bytes 655360 | tf_op jit(solution)/shard_map/all_gather | solution.py:88
  26.0 1.5 %pad_maximum_fusion = f32[4,64,1024]{2,0,1:T(4,128)} fusion(f32[2,64,1024]{2,0,1:T(2,128)S(1)} %all_gather.3, f32[2,64,1024]{2,0,1:T(2,128)S(1)} %bitcast.107), kind=kLoop, calls=%fused_computation.12 | loop fusion | flops 262144 | bytes 2097152 | tf_op jit(solution)/shard_map/concatenate | solution.py:90
  27.5 6.1 %all-to-all-start = ((f32[4,64,1024]{2,0,1:T(4,128)}), f32[4,64,1024]{2,0,1:T(4,128)S(1)}, u32[]{:S(2)}, u32[]{:S(2)}) async-start(f32[4,64,1024]{2,0,1:T(4,128)} %pad_maximum_fusion), calls=%async_computation | async-start | bytes 2097152 | tf_op jit(solution)/shard_map/all_to_all | solution.py:63
  35.3 0.7 fusion.8
  36.0 0.9 copy-done
  36.8 0.7 fusion.9
  37.6 0.9 copy-done.5
  38.4 1.3 convolution_add_fusion.2
  40.2 1.3 convolution_add_fusion.3
  41.5 18.5 %all-to-all-done = f32[4,64,1024]{2,0,1:T(4,128)S(1)} async-done(((f32[4,64,1024]{2,0,1:T(4,128)}), f32[4,64,1024]{2,0,1:T(4,128)S(1)}, u32[]{:S(2)}, u32[]{:S(2)}) %all-to-all-start) | async-done | bytes 1048608 | tf_op jit(solution)/shard_map/all_to_all | solution.py:63
  59.9 0.8 fusion.60
  61.8 1.2 copy-done.2
  63.1 0.7 fusion.6
  63.8 0.7 fusion.7
  64.6 0.7 fusion.10
  65.3 0.7 fusion.11
  66.0 0.9 copy-done.6
  67.3 1.1 copy-done.4
  69.0 0.7 fusion.24
  71.5 0.7 fusion.31
  73.1 0.7 copy.86
  73.8 29.5 %all_to_all.15 = f32[4,64,1024]{2,0,1:T(4,128)S(1)} all-to-all(f32[4,64,1024]{2,0,1:T(4,128)S(1)} %copy.86), channel_id=1, replica_groups=mesh['dp'=4,'seq'=8] {'seq'}, dimensions={1} | all-to-all | bytes 2097152 | tf_op jit(solution)/shard_map/all_to_all | solution.py:63
  103.3 1.1 slice.172
  106.1 0.7 copy.87
  107.1 0.7 copy.88
  107.8 28.3 %all-reduce.3.cloned.1.call-done = f32[2,64,1024]{2,0,1:T(2,128)} async-done(((f32[2,64,1024]{2,0,1:T(2,128)}), f32[2,64,1024]{2,0,1:T(2,128)}) %all-reduce.3.cloned.1.call-update) | async-done | bytes 524304
  136.1 0.9 constant_dynamic-slice_fusion
  137.0 0.7 copy.89
  (53 shorter events, 8.3 us)
Async XLA Ops:
  9.1 18.4 %all-to-all-start.1 = ((f32[1,64,1024]{2,0,1:T(1,128)}), f32[1,64,1024]{2,0,1:T(1,128)S(1)}, u32[]{:S(2)}, u32[]{:S(2)}) async-start(f32[1,64,1024]{2,0,1:T(1,128)} %fusion.20), calls=%async_computation.1 | async-start | bytes 524288 | tf_op jit(solution)/shard_map/all_to_all | solution.py:63
  26.0 7.7 %copy-start.12 = (f32[8,8,1]{1,0,2:T(8,128)S(1)}, f32[8,8,1]{1,0,2:T(8,128)}, u32[]{:S(2)}) copy-start(f32[8,8,1]{1,0,2:T(8,128)} %constant.34) | copy-start | bytes 772
  27.5 6.8 %copy-start.9 = (f32[8,1024]{1,0:T(8,128)S(1)}, f32[8,1024]{1,0:T(8,128)}, u32[]{:S(2)}) copy-start(f32[8,1024]{1,0:T(8,128)} %constant.29) | copy-start | bytes 98308
  27.5 6.8 %copy-start.10 = (f32[8,1024]{1,0:T(8,128)S(1)}, f32[8,1024]{1,0:T(8,128)}, u32[]{:S(2)}) copy-start(f32[8,1024]{1,0:T(8,128)} %constant.28) | copy-start | bytes 98308
  27.5 6.8 %copy-start.13 = (f32[8,8,1]{1,0,2:T(8,128)S(1)}, f32[8,8,1]{1,0,2:T(8,128)}, u32[]{:S(2)}) copy-start(f32[8,8,1]{1,0,2:T(8,128)} %constant.35) | copy-start | bytes 772
  27.5 32.4 %all-to-all-start = ((f32[4,64,1024]{2,0,1:T(4,128)}), f32[4,64,1024]{2,0,1:T(4,128)S(1)}, u32[]{:S(2)}, u32[]{:S(2)}) async-start(f32[4,64,1024]{2,0,1:T(4,128)} %pad_maximum_fusion), calls=%async_computation | async-start | bytes 2097152 | tf_op jit(solution)/shard_map/all_to_all | solution.py:63
  33.6 102.5 %all-reduce.3.cloned.1.call-start = ((), (), s32[]{:S(2)}) async-start(), calls=%async_computation.3 | async-start | bytes 1048576
  33.7 1.6 %copy-start.1 = (bf16[1024,1024]{1,0:T(8,128)(2,1)S(1)}, bf16[1024,1024]{1,0:T(8,128)(2,1)}, u32[]{:S(2)}) copy-start(bf16[1024,1024]{1,0:T(8,128)(2,1)} %constant.23.clone) | copy-start | bytes 6291460
  35.2 1.6 %copy-start = (bf16[1024,1024]{1,0:T(8,128)(2,1)S(1)}, bf16[1024,1024]{1,0:T(8,128)(2,1)}, u32[]{:S(2)}) copy-start(bf16[1024,1024]{1,0:T(8,128)(2,1)} %constant.21.clone) | copy-start | bytes 6291460
  36.8 1.6 %copy-start.5 = (bf16[1024,1024]{1,0:T(8,128)(2,1)S(1)}, bf16[1024,1024]{1,0:T(8,128)(2,1)}, u32[]{:S(2)}) copy-start(bf16[1024,1024]{1,0:T(8,128)(2,1)} %constant.24.clone) | copy-start | bytes 6291460
  38.4 1.8 %copy-start.3 = (bf16[1024,1024]{1,0:T(8,128)(2,1)S(1)}, bf16[1024,1024]{1,0:T(8,128)(2,1)}, u32[]{:S(2)}) copy-start(bf16[1024,1024]{1,0:T(8,128)(2,1)} %constant.22.clone) | copy-start | bytes 6291460
  59.9 1.0 copy-start.7
  59.9 1.2 copy-start.8
  61.5 1.6 %copy-start.2 = (bf16[1024,1024]{1,0:T(8,128)(2,1)S(1)}, bf16[1024,1024]{1,0:T(8,128)(2,1)}, u32[]{:S(2)}) copy-start(bf16[1024,1024]{1,0:T(8,128)(2,1)} %constant.23.clone) | copy-start | bytes 6291460
  65.3 1.6 %copy-start.6 = (bf16[1024,1024]{1,0:T(8,128)(2,1)S(1)}, bf16[1024,1024]{1,0:T(8,128)(2,1)}, u32[]{:S(2)}) copy-start(bf16[1024,1024]{1,0:T(8,128)(2,1)} %constant.24.clone) | copy-start | bytes 6291460
  66.9 1.6 %copy-start.4 = (bf16[1024,1024]{1,0:T(8,128)(2,1)S(1)}, bf16[1024,1024]{1,0:T(8,128)(2,1)}, u32[]{:S(2)}) copy-start(bf16[1024,1024]{1,0:T(8,128)(2,1)} %constant.22.clone) | copy-start | bytes 6291460
  73.8 30.6 %copy-start.14 = (u32[32]{0:T(128)S(1)}, u32[32]{0:T(128)}, u32[]{:S(2)}) copy-start(u32[32]{0:T(128)} %constant.32) | copy-start | bytes 388
  73.8 33.0 %copy-start.11 = (bf16[1,64,1024]{2,1,0:T(8,128)(2,1)S(1)}, bf16[1,64,1024]{2,1,0:T(8,128)(2,1)}, u32[]{:S(2)}) copy-start(bf16[1,64,1024]{2,1,0:T(8,128)(2,1)} %param.16) | copy-start | bytes 393220
Sparse Core Ops, SparseCore 0:
  104.5 31.5 all-reduce.2
where the time goes:
time: 145 us
  waiting for transfers between devices  46.8 us (32%)
  blocking collectives  36.6 us (25%)
  local copies, waits for them, and re-layouts  15.7 us (11%)
  between operations  15 us (10%)
  starting transfers between devices  13.5 us (9%)
  matrix products  12.3 us (8%)
  other arithmetic  4.7 us (3%)
    all_to_all x1, blocking collectives, exchange(): lax.all_to_all(blocks, 'seq', split_axis=1, concat_axis=1, tiled=True)  29.5 us
    unnamed x2, waiting for transfers between devices  28.3 us
    all_to_all x2, waiting for transfers between devices, exchange(): lax.all_to_all(blocks, 'seq', split_axis=1, concat_axis=1, tiled=True)  18.5 us
    all_to_all x2, starting transfers between devices, exchange(): lax.all_to_all(blocks, 'seq', split_axis=1, concat_axis=1, tiled=True)  13.4 us
    unnamed x38, local copies, waits for them, and re-layouts  12.1 us
    all_gather x1, blocking collectives, per_device_arrays(): filters = lax.all_gather(filter_spectrum, 'dp', axis=1, tiled=True)  7.17 us
    dot_general x6, matrix products, split_product(): rest = jnp.dot(high, table[1], preferred_element_type=jnp.float32)  4.3 us
    dot_general x6, matrix products, split_product(): jnp.dot(jnp.concatenate([high, low], axis=0), table[0], preferred_element...  4.26 us
  transfers between devices with their start and end apart: 3, of which 2 were waited for; matrix products, arithmetic and copies ran while one was open for 8% of the time, Pallas kernels for 0%

commit v1 on v0

--- a/solution.py
+++ b/solution.py
@@ -1,9 +1,12 @@
+import functools
 import math
 
 import jax
 import jax.numpy as jnp
 import numpy as np
 from jax import lax
+from jax.experimental import pallas as pl
+from jax.experimental.pallas import tpu as pltpu
 from jax.sharding import PartitionSpec as P
 
 
@@ -125,9 +128,341 @@
     )
 
 
+MESH = pl.DeviceIdType.MESH
+
+
+def weighted(terms):
+    total = None
+    for weight, value in terms:
+        if abs(weight) < 1e-12:
+            continue
+        if abs(abs(weight) - 1.0) < 1e-12:
+            if total is None:
+                total = value if weight > 0 else -value
+            else:
+                total = total + value if weight > 0 else total - value
+        else:
+            total = value * weight if total is None else total + value * weight
+    return total
+
+
+def kernel(
+    dp_count, seq_count, own, tile,
+    out_cot, gate, spectrum, filt, tw_cos, tw_sin, cos_hi, cos_lo, sin_hi, sin_lo,
+    grad_input, grad_gate, grad_filter,
+    tables, delta_out, delta_in, spec_in, filt_in, staged, split, spec_delta, local,
+    back_out, back_in, conv_out, conv_in, terms, terms_in, summed, owned,
+    table_sem, self_sem, delta_sem, spec_sem, filt_sem, spread_sem,
+    back_sem, conv_sem, terms_sem, owned_sem,
+):
+    dp = lax.axis_index("dp")
+    seq = lax.axis_index("seq")
+    group = seq_count // dp_count
+    positions = out_cot.shape[1]
+    rows = seq_count * own
+    home, place = seq // group, seq % group
+
+    table_copies = [
+        pltpu.make_async_copy(src, tables.at[i], table_sem.at[i])
+        for i, src in enumerate((cos_hi, sin_hi, cos_lo, sin_lo))
+    ]
+
+    def seq_peer(step):
+        return lax.rem(seq + step, seq_count)
+
+    def seq_exchange(source_of, target_of, sems, step):
+        to, come = seq_peer(step), seq_peer(seq_count - step)
+        make = lambda source, target: pltpu.make_async_remote_copy(
+            src_ref=source_of(source), dst_ref=target_of(target),
+            send_sem=sems.at[0, step], recv_sem=sems.at[1, step],
+            device_id={"dp": dp, "seq": to}, device_id_type=MESH,
+        )
+        return make(to, seq), make(to, come)
+
+    def dp_exchange(source_of, target_of, sems, step):
+        to, come = lax.rem(dp + step, dp_count), lax.rem(dp + dp_count - step, dp_count)
+        make = lambda source, target: pltpu.make_async_remote_copy(
+            src_ref=source_of(source), dst_ref=target_of(target),
+            send_sem=sems.at[0, step], recv_sem=sems.at[1, step],
+            device_id={"dp": to, "seq": seq}, device_id_type=MESH,
+        )
+        return make(to, dp), make(to, come)
+
+    class Swap:
+        def __init__(self, source_of, target_of, sems):
+            self.parts = []
+            for i in range(group):
+                own_part = (dp == home) & (place == i)
+                make = lambda slot, i=i: pltpu.make_async_remote_copy(
+                    src_ref=source_of(i), dst_ref=target_of(slot),
+                    send_sem=sems.at[0, i], recv_sem=sems.at[1, slot[1]],
+                    device_id={"dp": home, "seq": dp * group + i}, device_id_type=MESH,
+                )
+                here = pltpu.make_async_copy(
+                    source_of(i), target_of((seq, place)), sems.at[0, i]
+                )
+                self.parts.append(
+                    (own_part, make((seq, place)), make((dp * group + i, i)), here)
+                )
+
+        def start(self):
+            for own_part, sent, _, here in self.parts:
+                pl.when(own_part)(here.start)
+                pl.when(jnp.logical_not(own_part))(sent.start)
+
+        def wait_recv(self):
+            for own_part, _, got, here in self.parts:
+                pl.when(own_part)(here.wait)
+                pl.when(jnp.logical_not(own_part))(got.wait_recv)
+
+        def wait_send(self):
+            for own_part, sent, _, _ in self.parts:
+                pl.when(jnp.logical_not(own_part))(sent.wait_send)
+
+    steps = range(1, seq_count)
+    pending = []
+
+    upstream = out_cot[...].astype(jnp.float32)
+    delta_out[...] = (upstream * gate[...].astype(jnp.float32)).reshape(delta_out.shape)
+    delta_moves = [seq_exchange(lambda b: delta_out.at[b], lambda b: delta_in.at[b], delta_sem, k) for k in steps]
+    for sent, _ in delta_moves:
+        sent.start()
+        pending.append(sent)
+    filt_swap = Swap(
+        lambda i: filt.at[:, pl.ds(i * own, own), :],
+        lambda slot: filt_in.at[slot[0]],
+        filt_sem,
+    )
+    filt_swap.start()
+    block = lambda b: spectrum.at[:, pl.ds(pl.multiple_of(b * own, own), own), :]
+    spec_moves = [seq_exchange(block, lambda b: spec_in.at[:, b], spec_sem, k) for k in steps]
+    for sent, _ in spec_moves:
+        sent.start()
+        pending.append(sent)
+    spec_here = pltpu.make_async_copy(block(seq), spec_in.at[:, seq], self_sem.at[0])
+    spec_here.start()
+    for copy in table_copies:
+        copy.start()
+    delta_in[seq] = delta_out[seq]
+
+    filt_swap.wait_recv()
+    mine = lambda _: filt_in.at[pl.ds(dp * group, group)]
+    spread = []
+    for k in range(1, dp_count):
+        sent, _ = dp_exchange(mine, mine, spread_sem, k)
+        come = lax.rem(dp + dp_count - k, dp_count)
+        _, got = dp_exchange(mine, lambda _, come=come: filt_in.at[pl.ds(come * group, group)], spread_sem, k)
+        sent.start()
+        pending.append(sent)
+        spread.append(got)
+
+    half = seq_count // 2
+    angle = 2.0 * math.pi / seq_count
+
+    def cos_of(n):
+        return math.cos(angle * (n % seq_count))
+
+    def sin_of(n):
+        return math.sin(angle * (n % seq_count))
+
+    def put(freq, real, imag):
+        staged[freq * own : (freq + 1) * own] = real
+        staged[rows + freq * own : rows + (freq + 1) * own] = imag
+
+    def transform(target, sign):
+        values = staged[...]
+        high = values.astype(jnp.bfloat16)
+        split[: 2 * rows] = high
+        split[2 * rows :] = (values - high.astype(jnp.float32)).astype(jnp.bfloat16)
+
+        def one(j, carry):
+            columns = pl.ds(pl.multiple_of(j * tile, tile), tile)
+
+            def product(high_at, low_at):
+                both = jnp.dot(split[...], tables[high_at, :, columns], preferred_element_type=jnp.float32)
+                rest = jnp.dot(split[: 2 * rows], tables[low_at, :, columns], preferred_element_type=jnp.float32)
+                return both[: 2 * rows] + both[2 * rows :] + rest
+
+            by_cos = product(0, 2)
+            by_sin = product(1, 3)
+            if sign > 0:
+                target[0, :, columns] = by_cos[:rows] - by_sin[rows:]
+                target[1, :, columns] = by_cos[rows:] + by_sin[:rows]
+            else:
+                target[0, :, columns] = by_cos[:rows] + by_sin[rows:]
+                target[1, :, columns] = by_cos[rows:] - by_sin[:rows]
+            return carry
+
+        lax.fori_loop(0, positions // tile, one, 0)
+
+    def inverse(target):
+        transform(local, 1)
+        real, imag = [], []
+        for f in range(seq_count):
+            a = local[0, f * own : (f + 1) * own]
+            b = local[1, f * own : (f + 1) * own]
+            c, s = tw_cos[f : f + 1], tw_sin[f : f + 1]
+            real.append(a * c - b * s)
+            imag.append(b * c + a * s)
+        pairs = [
+            (f, real[f] + real[seq_count - f], imag[f] - imag[seq_count - f])
+            for f in range(1, half)
+        ]
+        for p in range(seq_count):
+            parts = [(1.0, real[0]), (cos_of(p * half), real[half])]
+            for f, a, b in pairs:
+                parts += [(cos_of(p * f), a), (-sin_of(p * f), b)]
+            target[p] = weighted(parts)
+
+    for _, got in delta_moves:
+        got.wait_recv()
+    blocks = [delta_in[p] for p in range(seq_count)]
+    for f in range(half + 1):
+        real = weighted([(cos_of(p * f), blocks[p]) for p in range(seq_count)])
+        imag = weighted([(-sin_of(p * f), blocks[p]) for p in range(seq_count)])
+        for g, turn in {f: 1.0, (seq_count - f) % seq_count: -1.0 if f % half else 1.0}.items():
+            c, s = tw_cos[g : g + 1], tw_sin[g : g + 1]
+            if imag is None:
+                put(g, real * c, -(real * s))
+            else:
+                b = imag if turn > 0 else -imag
+                put(g, real * c + b * s, b * c - real * s)
+    for copy in table_copies:
+        copy.wait()
+    transform(spec_delta, -1)
+
+    for got in spread:
+        got.wait_recv()
+    for f in range(seq_count):
+        a, b = filt_in[f, 0], filt_in[f, 1]
+        c = spec_delta[0, f * own : (f + 1) * own]
+        d = spec_delta[1, f * own : (f + 1) * own]
+        put(f, a * c + b * d, a * d - b * c)
+    inverse(back_out)
+    back_moves = [seq_exchange(lambda b: back_out.at[b], lambda b: back_in.at[b], back_sem, k) for k in steps]
+    for sent, _ in back_moves:
+        sent.start()
+        pending.append(sent)
+    back_in[seq] = back_out[seq]
+
+    spec_here.wait()
+    for _, got in spec_moves:
+        got.wait_recv()
+    for f in range(seq_count):
+        a, b = spec_in[0, f], spec_in[1, f]
+        c = spec_delta[0, f * own : (f + 1) * own]
+        d = spec_delta[1, f * own : (f + 1) * own]
+        terms[f, 0] = a * c + b * d
+        terms[f, 1] = a * d - b * c
+        c, d = filt_in[f, 0], filt_in[f, 1]
+        put(f, a * c - b * d, a * d + b * c)
+    quarter = lambda h: terms.at[pl.ds(h * group, group)]
+    terms_moves = []
+    for k in range(1, dp_count):
+        sent, _ = dp_exchange(quarter, lambda _, k=k: terms_in.at[k - 1], terms_sem, k)
+        sent.start()
+        pending.append(sent)
+        terms_moves.append(sent)
+    inverse(conv_out)
+    conv_moves = [seq_exchange(lambda b: conv_out.at[b], lambda b: conv_in.at[b], conv_sem, k) for k in steps]
+    for sent, _ in conv_moves:
+        sent.start()
+        pending.append(sent)
+    conv_in[seq] = conv_out[seq]
+
+    for move in terms_moves:
+        move.wait_recv()
+    total = terms[pl.ds(dp * group, group)]
+    for k in range(dp_count - 1):
+        total = total + terms_in[k]
+    summed[...] = total
+    owned_swap = Swap(lambda i: summed.at[i], lambda slot: owned.at[slot[1]], owned_sem)
+    owned_swap.start()
+
+    for _, got in back_moves:
+        got.wait_recv()
+    grad_input[...] = back_in[...].reshape(rows, positions).astype(jnp.bfloat16)
+    for _, got in conv_moves:
+        got.wait_recv()
+    upstream = out_cot[...].astype(jnp.float32)
+    grad_gate[...] = (upstream * conv_in[...].reshape(rows, positions)).astype(jnp.bfloat16)
+    owned_swap.wait_recv()
+    for i in range(group):
+        grad_filter[:, i * own : (i + 1) * own] = owned[i]
+    for sent in pending:
+        sent.wait_send()
+    filt_swap.wait_send()
+    owned_swap.wait_send()
+
+
+def fused(grad_out, gate, input_spectrum, filter_spectrum, tables, dp_count, seq_count):
+    _, channels, positions = grad_out.shape
+    own = channels // seq_count
+    group = seq_count // dp_count
+    (cos_hi, cos_lo), (sin_hi, sin_lo), (tw_cos, tw_sin), _ = tables
+    vmem = pl.BlockSpec(memory_space=pltpu.VMEM)
+    anywhere = pl.BlockSpec(memory_space=pl.ANY)
+    single = jnp.float32
+    blocks = (seq_count, own, positions)
+    pair = lambda count: pltpu.SemaphoreType.DMA((2, count))
+    back, gated, filt = pl.pallas_call(
+        functools.partial(kernel, dp_count, seq_count, own, min(256, positions)),
+        out_shape=(
+            jax.ShapeDtypeStruct((channels, positions), jnp.bfloat16),
+            jax.ShapeDtypeStruct((channels, positions), jnp.bfloat16),
+            jax.ShapeDtypeStruct(filter_spectrum.shape, single),
+        ),
+        in_specs=[vmem, vmem, anywhere, anywhere, vmem, vmem] + [anywhere] * 4,
+        out_specs=(vmem, vmem, vmem),
+        scratch_shapes=[
+            pltpu.VMEM((4, positions, positions), jnp.bfloat16),
+            pltpu.VMEM(blocks, single),
+            pltpu.VMEM(blocks, single),
+            pltpu.VMEM((2,) + blocks, single),
+            pltpu.VMEM((seq_count, 2, own, positions), single),
+            pltpu.VMEM((2 * channels, positions), single),
+            pltpu.VMEM((4 * channels, positions), jnp.bfloat16),
+            pltpu.VMEM((2, channels, positions), single),
+            pltpu.VMEM((2, channels, positions), single),
+            pltpu.VMEM(blocks, single),
+            pltpu.VMEM(blocks, single),
+            pltpu.VMEM(blocks, single),
+            pltpu.VMEM(blocks, single),
+            pltpu.VMEM((seq_count, 2, own, positions), single),
+            pltpu.VMEM((dp_count - 1, group, 2, own, positions), single),
+            pltpu.VMEM((group, 2, own, positions), single),
+            pltpu.VMEM((group, 2, own, positions), single),
+            pltpu.SemaphoreType.DMA((4,)),
+            pltpu.SemaphoreType.DMA((1,)),
+            pair(seq_count),
+            pair(seq_count),
+            pair(group),
+            pair(dp_count),
+            pair(seq_count),
+            pair(seq_count),
+            pair(dp_count),
+            pair(group),
+        ],
+        compiler_params=pltpu.CompilerParams(
+            has_side_effects=True, vmem_limit_bytes=48 * 1024 * 1024
+        ),
+    )(
+        grad_out[0], gate[0], input_spectrum[0], filter_spectrum, tw_cos, tw_sin,
+        cos_hi, cos_lo, sin_hi, sin_lo,
+    )
+    return back[None], gated[None], filt
+
+
 def solution(mesh):
     def per_device(grad_out, gate, input_spectrum, filter_spectrum):
         tables = host_tables(mesh.shape["seq"], grad_out.shape[2])
+        batch, channels, positions = grad_out.shape
+        dp_count, seq_count = mesh.shape["dp"], mesh.shape["seq"]
+        aligned = channels % (8 * seq_count) == 0 and positions % 128 == 0
+        if batch == 1 and aligned and seq_count % (2 * dp_count) == 0:
+            return fused(
+                grad_out, gate, input_spectrum, filter_spectrum, tables, dp_count, seq_count
+            )
         return per_device_arrays(grad_out, gate, input_spectrum, filter_spectrum, tables)
 
     return jax.shard_map(

time: 145 us -> 62.2 us (0.43)
  the two profiles are of different devices: /device:TPU:0 before, /device:TPU:6 now
where the time goes in v1:
time: 62.2 us; the launch traced here: 61.8 us
  Pallas kernels  50.8 us (82%)
  local copies, waits for them, and re-layouts  10.4 us (17%)
  between operations  0.66 us (1%)
    pallas_call x1, Pallas kernels, fused(): pl.pallas_call(functools.partial(kernel, dp_count, seq_count, own, min(25...  50.8 us
    unnamed x19, local copies, waits for them, and re-layouts  10.4 us

profile of v1, /device:TPU:6, one launch (start us, length us, event | category | flops | bytes accessed | tf_op | source)
XLA Modules:
  0.0 61.8 jit_solution(8596779118933744742)
XLA Ops:
  0.6 0.0 copy-start
  0.6 1.6 %copy-done = bf16[1024,1024]{1,0:T(8,128)(2,1)S(1)} copy-done((bf16[1024,1024]{1,0:T(8,128)(2,1)S(1)}, bf16[1024,1024]{1,0:T(8,128)(2,1)}, u32[]{:S(2)}) %copy-start) | copy-done | bytes 2097176
  2.2 0.0 copy-start.1
  2.2 1.6 %copy-done.1 = bf16[1024,1024]{1,0:T(8,128)(2,1)S(1)} copy-done((bf16[1024,1024]{1,0:T(8,128)(2,1)S(1)}, bf16[1024,1024]{1,0:T(8,128)(2,1)}, u32[]{:S(2)}) %copy-start.1) | copy-done | bytes 2097176
  3.8 0.0 copy-start.2
  3.8 1.0 %copy-done.2 = f32[1,2,64,1024]{3,2,1,0:T(8,128)S(1)} copy-done((f32[1,2,64,1024]{3,2,1,0:T(8,128)S(1)}, f32[1,2,64,1024]{3,2,1,0:T(8,128)}, u32[]{:S(2)}) %copy-start.2) | copy-done | bytes 524312
  4.9 0.0 copy-start.3
  4.9 0.9 %copy-done.3 = bf16[1,64,1024]{2,1,0:T(8,128)(2,1)S(1)} copy-done((bf16[1,64,1024]{2,1,0:T(8,128)(2,1)S(1)}, bf16[1,64,1024]{2,1,0:T(8,128)(2,1)}, u32[]{:S(2)}) %copy-start.3) | copy-done | bytes 131096
  5.8 0.0 copy-start.4
  5.8 0.9 %copy-done.4 = bf16[1,64,1024]{2,1,0:T(8,128)(2,1)S(1)} copy-done((bf16[1,64,1024]{2,1,0:T(8,128)(2,1)S(1)}, bf16[1,64,1024]{2,1,0:T(8,128)(2,1)}, u32[]{:S(2)}) %copy-start.4) | copy-done | bytes 131096
  6.7 0.0 copy-start.5
  6.7 0.9 %copy-done.5 = f32[2,16,1024]{2,1,0:T(8,128)S(1)} copy-done((f32[2,16,1024]{2,1,0:T(8,128)S(1)}, f32[2,16,1024]{2,1,0:T(8,128)}, u32[]{:S(2)}) %copy-start.5) | copy-done | bytes 131096
  7.6 0.0 copy-start.6
  7.6 0.8 %copy-done.6 = f32[8,1024]{1,0:T(8,128)S(1)} copy-done((f32[8,1024]{1,0:T(8,128)S(1)}, f32[8,1024]{1,0:T(8,128)}, u32[]{:S(2)}) %copy-start.6) | copy-done | bytes 32792
  8.3 0.0 copy-start.7
  8.3 0.8 %copy-done.7 = f32[8,1024]{1,0:T(8,128)S(1)} copy-done((f32[8,1024]{1,0:T(8,128)S(1)}, f32[8,1024]{1,0:T(8,128)}, u32[]{:S(2)}) %copy-start.7) | copy-done | bytes 32792
  9.1 50.8 %shard_map.121 = (bf16[64,1024]{1,0:T(8,128)(2,1)S(1)}, bf16[64,1024]{1,0:T(8,128)(2,1)S(1)}, f32[2,16,1024]{2,1,0:T(8,128)S(1)}) custom-call(bf16[64,1024]{1,0:T(8,128)(2,1)S(1)} %bitcast.6, bf16[64,1024]{1,0:T(8,128)(2,1)S(1)} %bitcast.7, f32[2,64,1024]{2,1,0:T(8,128)S(1)} %bitcast.5, f32[2,16,1024]{2,1,0:T(8,128)S(1)} %copy-done.5, ...), custom_call_target="tpu_custom_call" | custom-call | tf_op jit(solution)/shard_map/pallas_call | solution.py:408
  59.8 0.7 %copy.16 = bf16[1,64,1024]{2,1,0:T(8,128)(2,1)} copy(bf16[1,64,1024]{2,1,0:T(8,128)(2,1)S(1)} %bitcast.9) | data formatting | bytes 262144
  60.5 0.7 %copy.17 = bf16[1,64,1024]{2,1,0:T(8,128)(2,1)} copy(bf16[1,64,1024]{2,1,0:T(8,128)(2,1)S(1)} %bitcast.8) | data formatting | bytes 262144
  61.2 0.7 %copy.18 = f32[2,16,1024]{2,1,0:T(8,128)} copy(f32[2,16,1024]{2,1,0:T(8,128)S(1)} %get-tuple-element.14) | data formatting | bytes 262144
Async XLA Ops:
  0.6 1.6 %copy-start = (bf16[1024,1024]{1,0:T(8,128)(2,1)S(1)}, bf16[1024,1024]{1,0:T(8,128)(2,1)}, u32[]{:S(2)}) copy-start(bf16[1024,1024]{1,0:T(8,128)(2,1)} %constant.15.clone.cos_lo) | copy-start | bytes 6291460
  2.2 1.6 %copy-start.1 = (bf16[1024,1024]{1,0:T(8,128)(2,1)S(1)}, bf16[1024,1024]{1,0:T(8,128)(2,1)}, u32[]{:S(2)}) copy-start(bf16[1024,1024]{1,0:T(8,128)(2,1)} %constant.14.clone.cos_hi) | copy-start | bytes 6291460
  3.8 1.0 %copy-start.2 = (f32[1,2,64,1024]{3,2,1,0:T(8,128)S(1)}, f32[1,2,64,1024]{3,2,1,0:T(8,128)}, u32[]{:S(2)}) copy-start(f32[1,2,64,1024]{3,2,1,0:T(8,128)} %param.12) | copy-start | bytes 1572868
  4.9 0.9 %copy-start.3 = (bf16[1,64,1024]{2,1,0:T(8,128)(2,1)S(1)}, bf16[1,64,1024]{2,1,0:T(8,128)(2,1)}, u32[]{:S(2)}) copy-start(bf16[1,64,1024]{2,1,0:T(8,128)(2,1)} %param.10) | copy-start | bytes 393220
  5.8 0.9 %copy-start.4 = (bf16[1,64,1024]{2,1,0:T(8,128)(2,1)S(1)}, bf16[1,64,1024]{2,1,0:T(8,128)(2,1)}, u32[]{:S(2)}) copy-start(bf16[1,64,1024]{2,1,0:T(8,128)(2,1)} %param.11) | copy-start | bytes 393220
  6.7 0.9 %copy-start.5 = (f32[2,16,1024]{2,1,0:T(8,128)S(1)}, f32[2,16,1024]{2,1,0:T(8,128)}, u32[]{:S(2)}) copy-start(f32[2,16,1024]{2,1,0:T(8,128)} %filt.1) | copy-start | bytes 393220
  7.6 0.8 %copy-start.6 = (f32[8,1024]{1,0:T(8,128)S(1)}, f32[8,1024]{1,0:T(8,128)}, u32[]{:S(2)}) copy-start(f32[8,1024]{1,0:T(8,128)} %constant.13.clone.tw_sin) | copy-start | bytes 98308
  8.3 0.8 %copy-start.7 = (f32[8,1024]{1,0:T(8,128)S(1)}, f32[8,1024]{1,0:T(8,128)}, u32[]{:S(2)}) copy-start(f32[8,1024]{1,0:T(8,128)} %constant.12.clone.tw_cos) | copy-start | bytes 98308

commit v2 on v1

--- a/solution.py
+++ b/solution.py
@@ -148,9 +148,9 @@
 
 def kernel(
     dp_count, seq_count, own, tile,
-    out_cot, gate, spectrum, filt, tw_cos, tw_sin, cos_hi, cos_lo, sin_hi, sin_lo,
+    cot_home, gate_home, spectrum, filt, cos_home, sin_home, cos_hi, cos_lo, sin_hi, sin_lo,
     grad_input, grad_gate, grad_filter,
-    tables, delta_out, delta_in, spec_in, filt_in, staged, split, spec_delta, local,
+    out_cot, gate, tw_cos, tw_sin, tables, delta_out, delta_in, spec_in, filt_in, staged, split, spec_delta, local,
     back_out, back_in, conv_out, conv_in, terms, terms_in, summed, owned,
     table_sem, self_sem, delta_sem, spec_sem, filt_sem, spread_sem,
     back_sem, conv_sem, terms_sem, owned_sem,
@@ -158,7 +158,7 @@
     dp = lax.axis_index("dp")
     seq = lax.axis_index("seq")
     group = seq_count // dp_count
-    positions = out_cot.shape[1]
+    positions = cot_home.shape[1]
     rows = seq_count * own
     home, place = seq // group, seq % group
 
@@ -166,6 +166,36 @@
         pltpu.make_async_copy(src, tables.at[i], table_sem.at[i])
         for i, src in enumerate((cos_hi, sin_hi, cos_lo, sin_lo))
     ]
+
+    early = [
+        pltpu.make_async_copy(src, dst, self_sem.at[1 + i])
+        for i, (src, dst) in enumerate(
+            ((cot_home, out_cot), (gate_home, gate), (cos_home, tw_cos), (sin_home, tw_sin))
+        )
+    ]
+    for copy in early:
+        copy.start()
+    barrier = pltpu.get_barrier_semaphore()
+
+    def greet(dp_to, seq_to):
+        pl.semaphore_signal(
+            barrier, inc=1, device_id={"dp": dp_to, "seq": seq_to}, device_id_type=MESH
+        )
+
+    for k in range(1, seq_count):
+        greet(dp, lax.rem(seq + k, seq_count))
+    for k in range(1, dp_count):
+        greet(lax.rem(dp + k, dp_count), seq)
+    among = jnp.int32(0)
+    for i in range(group):
+        own_part = (dp == home) & (place == i)
+        pl.when(jnp.logical_not(own_part))(functools.partial(greet, home, dp * group + i))
+        among = among + own_part.astype(jnp.int32)
+    for copy in early:
+        copy.wait()
+    upstream = out_cot[...].astype(jnp.float32)
+    delta_out[...] = (upstream * gate[...].astype(jnp.float32)).reshape(delta_out.shape)
+    pl.semaphore_wait(barrier, seq_count - 1 + dp_count - 1 + group - among)
 
     def seq_peer(step):
         return lax.rem(seq + step, seq_count)
@@ -222,8 +252,6 @@
     steps = range(1, seq_count)
     pending = []
 
-    upstream = out_cot[...].astype(jnp.float32)
-    delta_out[...] = (upstream * gate[...].astype(jnp.float32)).reshape(delta_out.shape)
     delta_moves = [seq_exchange(lambda b: delta_out.at[b], lambda b: delta_in.at[b], delta_sem, k) for k in steps]
     for sent, _ in delta_moves:
         sent.start()
@@ -236,15 +264,17 @@
     filt_swap.start()
     block = lambda b: spectrum.at[:, pl.ds(pl.multiple_of(b * own, own), own), :]
     spec_moves = [seq_exchange(block, lambda b: spec_in.at[:, b], spec_sem, k) for k in steps]
-    for sent, _ in spec_moves:
-        sent.start()
-        pending.append(sent)
     spec_here = pltpu.make_async_copy(block(seq), spec_in.at[:, seq], self_sem.at[0])
     spec_here.start()
     for copy in table_copies:
         copy.start()
     delta_in[seq] = delta_out[seq]
-
+    for _, got in delta_moves:
+        got.wait_recv()
+
+    for sent, _ in spec_moves:
+        sent.start()
+        pending.append(sent)
     filt_swap.wait_recv()
     mine = lambda _: filt_in.at[pl.ds(dp * group, group)]
     spread = []
@@ -314,8 +344,6 @@
                 parts += [(cos_of(p * f), a), (-sin_of(p * f), b)]
             target[p] = weighted(parts)
 
-    for _, got in delta_moves:
-        got.wait_recv()
     blocks = [delta_in[p] for p in range(seq_count)]
     for f in range(half + 1):
         real = weighted([(cos_of(p * f), blocks[p]) for p in range(seq_count)])
@@ -401,7 +429,7 @@
     group = seq_count // dp_count
     (cos_hi, cos_lo), (sin_hi, sin_lo), (tw_cos, tw_sin), _ = tables
     vmem = pl.BlockSpec(memory_space=pltpu.VMEM)
-    anywhere = pl.BlockSpec(memory_space=pl.ANY)
+    far = pl.BlockSpec(memory_space=pltpu.HBM)
     single = jnp.float32
     blocks = (seq_count, own, positions)
     pair = lambda count: pltpu.SemaphoreType.DMA((2, count))
@@ -412,9 +440,13 @@
             jax.ShapeDtypeStruct((channels, positions), jnp.bfloat16),
             jax.ShapeDtypeStruct(filter_spectrum.shape, single),
         ),
-        in_specs=[vmem, vmem, anywhere, anywhere, vmem, vmem] + [anywhere] * 4,
+        in_specs=[far] * 10,
         out_specs=(vmem, vmem, vmem),
         scratch_shapes=[
+            pltpu.VMEM((channels, positions), jnp.bfloat16),
+            pltpu.VMEM((channels, positions), jnp.bfloat16),
+            pltpu.VMEM((seq_count, positions), single),
+            pltpu.VMEM((seq_count, positions), single),
             pltpu.VMEM((4, positions, positions), jnp.bfloat16),
             pltpu.VMEM(blocks, single),
             pltpu.VMEM(blocks, single),
@@ -433,7 +465,7 @@
             pltpu.VMEM((group, 2, own, positions), single),
             pltpu.VMEM((group, 2, own, positions), single),
             pltpu.SemaphoreType.DMA((4,)),
-            pltpu.SemaphoreType.DMA((1,)),
+            pltpu.SemaphoreType.DMA((5,)),
             pair(seq_count),
             pair(seq_count),
             pair(group),
@@ -444,7 +476,7 @@
             pair(group),
         ],
         compiler_params=pltpu.CompilerParams(
-            has_side_effects=True, vmem_limit_bytes=48 * 1024 * 1024
+            collective_id=0, has_side_effects=True, vmem_limit_bytes=56 * 1024 * 1024
         ),
     )(
         grad_out[0], gate[0], input_spectrum[0], filter_spectrum, tw_cos, tw_sin,

time: 62.2 us -> 53.7 us (0.86)
  the two profiles are of different devices: /device:TPU:6 before, /device:TPU:21 now
where the time goes in v2:
time: 53.7 us; the launch traced here: 53.5 us
  Pallas kernels  48.2 us (90%)
  local copies, waits for them, and re-layouts  4.7 us (9%)
  between operations  0.64 us (1%)
    pallas_call x1, Pallas kernels, fused(): pl.pallas_call(functools.partial(kernel, dp_count, seq_count, own, min(25...  48.2 us
    unnamed x3, local copies, waits for them, and re-layouts  4.7 us

profile of v2, /device:TPU:21, one launch (start us, length us, event | category | flops | bytes accessed | tf_op | source)
XLA Modules:
  0.0 53.5 jit_solution(17349576987267214888)
XLA Ops:
  0.6 48.2 %shard_map.121 = (bf16[64,1024]{1,0:T(8,128)(2,1)}, bf16[64,1024]{1,0:T(8,128)(2,1)}, f32[2,16,1024]{2,1,0:T(8,128)}) custom-call(bf16[64,1024]{1,0:T(8,128)(2,1)} %bitcast.6, bf16[64,1024]{1,0:T(8,128)(2,1)} %bitcast.7, f32[2,64,1024]{2,1,0:T(8,128)} %bitcast.5, f32[2,16,1024]{2,1,0:T(8,128)} %filt.1, f32[8,1024]{1,0:T(8,128)} %constant.12.clone.cos_home, ...), custom_call_target="tpu_custom_call" | custom-call | tf_op jit(solution)/shard_map/pallas_call | solution.py:436
  48.8 1.6 %copy.16 = bf16[1,64,1024]{2,1,0:T(8,128)(2,1)} copy(bf16[1,64,1024]{2,1,0:T(8,128)(2,1)} %bitcast.9) | data formatting | bytes 262144
  50.4 1.6 %copy.17 = bf16[1,64,1024]{2,1,0:T(8,128)(2,1)} copy(bf16[1,64,1024]{2,1,0:T(8,128)(2,1)} %bitcast.8) | data formatting | bytes 262144
  51.9 1.6 %copy.18 = f32[2,16,1024]{2,1,0:T(8,128)} copy(f32[2,16,1024]{2,1,0:T(8,128)} %get-tuple-element.14) | data formatting | bytes 262144
